TPU v7x, 256 devices: a whole 4x4x8 slice. The times are simulated.
256 devices in a mesh: mass: 128 (over x, z, y), rep: 2 (over core).
Axes of the slice: x: 4, y: 4, z: 8, core: 2. Of those that a mesh axis runs over, the one named last changes fastest.
Arguments:
- spectra: bfloat16 [131072, 1024], P(('mass', 'rep')), may hold values from -200 to 200
- window: int32 [131072], P(('mass', 'rep')), may hold values from 0 to 127, as said below
- labels: int32 [131072], P(('mass', 'rep')), may hold values from 0 to 63
- edge_labels: int32 [131072], P(('mass', 'rep')), may hold values from -1 to 63, as said below
Outputs:
- consensus: bfloat16 [8192, 1024], P('mass', 'rep')
- assigned: bfloat16 [131072, 1024], P(('mass', 'rep'))
Inputs may be any that keep to these rules, and one draw needn't show every extreme that they name: A file shard's 512 spectra hold between 0 and 8 of any one window. At least one window, the same in every file shard, gets exactly 8 from every file shard, so a window holds at most 2048 spectra in all; other windows may get fewer. A file shard holds between 0 and 1 spectra with edge_labels >= 0 of any one window. At least one window, the same in every file shard, gets exactly 1 such spectra from every file shard, so a window holds at most 256 of them; other windows may get fewer.
All inputs are finite; a program needn't handle non-finite values.
Results may differ from a plain program's by a relative error of at most 0.0033.
Values may be sent and summed in bfloat16 or wider, within the bound.
A program may use at most 64 MiB of HBM per device.

v0:
```python
import jax
import jax.numpy as jnp
from jax import lax
from jax.sharding import PartitionSpec as P

CLUSTERS = 64
CAP_MIN = 8


BETA = 6.0


def passed_along(block, axis, distance):
    devices = range(lax.axis_size(axis))
    route = [(i - distance, i) for i in devices if i - distance in devices]
    return lax.ppermute(block, axis, route)


def edge_pack(rows_in, edges_in, room):
    is_edge = edges_in >= 0
    position = jnp.cumsum(is_edge.astype(jnp.int32)) - 1
    picked = (position[None, :] == jnp.arange(room, dtype=jnp.int32)[:, None]) & is_edge[None, :]
    packed = jnp.dot(
        picked.astype(jnp.bfloat16), rows_in, preferred_element_type=jnp.float32
    ).astype(jnp.bfloat16)
    edge_code = jnp.sum(jnp.where(picked, edges_in[None, :] + 1, 0), axis=1).astype(jnp.int32)
    return (packed, edge_code)


def density_of(query_rows, query_labels, cand_rows, cand_labels):
    scores = (
        lax.dot_general(
            query_rows, cand_rows, (((1,), (1,)), ((), ())), preferred_element_type=jnp.float32
        )
        / query_rows.shape[1]
    )
    same_cluster = query_labels[:, None] == cand_labels[None, :]
    return jnp.sum(jnp.where(same_cluster, jnp.exp(BETA * (scores - 1.0)), 0.0), axis=1)


def body(spectra, window, labels, edge_labels):
    rows_here, dim_width = spectra.shape
    windows = lax.axis_size("mass")
    halves = lax.axis_size("rep")
    capacity = max(CAP_MIN, 2 * rows_here // windows)
    edge_slots = windows * max(1, capacity // 8)
    total_slots = windows * capacity
    widened = spectra.astype(jnp.float32)
    unit_rows = (
        widened * lax.rsqrt(jnp.mean(widened * widened, axis=1, keepdims=True) + 1e-06)
    ).astype(jnp.bfloat16)
    target = window[:, None] == jnp.arange(windows, dtype=jnp.int32)[None, :]
    earlier = jnp.cumsum(target.astype(jnp.int32), axis=0)
    rank_in = jnp.sum(jnp.where(target, earlier, 0), axis=1) - 1
    slot_of = window * capacity + rank_in
    send_rows = jnp.zeros((total_slots, dim_width), jnp.bfloat16).at[slot_of].set(unit_rows)
    send_labels = jnp.full((total_slots,), -1, jnp.int32).at[slot_of].set(labels)
    send_edges = jnp.full((total_slots,), -1, jnp.int32).at[slot_of].set(edge_labels)
    pair_rows, pair_labels, pair_edges = (
        lax.all_gather(send_rows.reshape(windows, capacity, dim_width), "rep", axis=1, tiled=True),
        lax.all_gather(send_labels.reshape(windows, capacity), "rep", axis=1, tiled=True),
        lax.all_gather(send_edges.reshape(windows, capacity), "rep", axis=1, tiled=True),
    )
    got_rows, got_labels, got_edges = (
        lax.all_to_all(pair_rows, "mass", split_axis=0, concat_axis=0, tiled=True),
        lax.all_to_all(pair_labels, "mass", split_axis=0, concat_axis=0, tiled=True),
        lax.all_to_all(pair_edges, "mass", split_axis=0, concat_axis=0, tiled=True),
    )
    rep_index = lax.axis_index("rep")
    all_rows = got_rows.reshape(windows * halves * capacity, dim_width)
    all_labels = got_labels.reshape(windows * halves * capacity)
    all_edges = got_edges.reshape(windows * halves * capacity)
    own_rows = lax.dynamic_index_in_dim(
        got_rows.reshape(windows, halves, capacity, dim_width), rep_index, 1, False
    ).reshape(total_slots, dim_width)
    own_labels = lax.dynamic_index_in_dim(
        got_labels.reshape(windows, halves, capacity), rep_index, 1, False
    ).reshape(total_slots)
    packed, edge_code = edge_pack(all_rows, all_edges, halves * edge_slots)
    edge_rows, edge_codes = passed_along((packed, edge_code), "mass", -1)
    density = density_of(own_rows, own_labels, all_rows, all_labels) + density_of(
        own_rows, own_labels, edge_rows, edge_codes - 1
    )
    cluster_ids = jnp.arange(CLUSTERS, dtype=jnp.int32)
    member = own_labels[None, :] == cluster_ids[:, None]
    weighted = (density[:, None] * own_rows.astype(jnp.float32)).astype(jnp.bfloat16)
    numerator = jnp.dot(member.astype(jnp.bfloat16), weighted, preferred_element_type=jnp.float32)
    member_count = jnp.sum(member.astype(jnp.float32), axis=1)
    share_width = dim_width // halves
    numerator, member_count = lax.psum((numerator, member_count), "rep")
    full_table = (numerator / (member_count + 1.0)[:, None]).astype(jnp.bfloat16)
    consensus = lax.dynamic_slice_in_dim(
        full_table, lax.axis_index("rep") * share_width, share_width, 1
    )
    chosen = own_labels[:, None] == cluster_ids[None, :]
    answers = jnp.dot(
        chosen.astype(jnp.bfloat16), full_table, preferred_element_type=jnp.float32
    ).astype(jnp.bfloat16)
    returned = lax.all_to_all(answers, "mass", split_axis=0, concat_axis=0, tiled=True)
    assigned = returned[slot_of]
    return (consensus, assigned)


def solution(mesh):
    placed = (P(("mass", "rep"), None), P(("mass", "rep")), P(("mass", "rep")), P(("mass", "rep")))
    return jax.shard_map(
        body,
        mesh=mesh,
        in_specs=placed,
        out_specs=(P("mass", "rep"), P(("mass", "rep"), None)),
        check_vma=False,
    )
```

profile of v0, /device:TPU:1, one launch (start us, length us, event | category | flops | bytes accessed | tf_op | source)
XLA Modules:
  0.0 297.9 jit_solution(17662792978549768040)
XLA Ops:
  7.2 0.8 copy.18
  8.3 0.9 fusion.37
  9.2 0.7 compare_select_fusion
  9.9 1.5 fusion
  11.4 4.9 %scatter_custom_fusion.1 = bf16[1024,1024]{1,0:T(8,128)(2,1)} fusion(s32[512]{0:T(512)S(1)} %compare_select_fusion, bf16[512,1024]{1,0:T(8,128)(2,1)} %param.4, f32[512]{0:T(512)S(1)} %add_rsqrt_fusion, bf16[]{:T(256)} %constant.23.clone.1), kind=kCustom, calls=%fused_computation.29 | custom fusion | flops 1572864 | bytes 3147778 | tf_op jit(solution)/shard_map/scatter | solution.py:56
  16.3 2.6 scatter_custom_fusion
  19.1 4.7 %all_gather.9 = s32[128,16]{0,1:T(8,128)S(1)} all-gather(s32[128,8]{0,1:T(8,128)S(1)} %copy.20), channel_id=1, replica_groups=mesh['mass'=128,'rep'=2] {'rep'}, dimensions={1}, use_global_device_ids=true | all-gather | bytes 12288 | tf_op jit(solution)/shard_map/all_gather | solution.py:61
  23.8 0.7 copy.21
  24.6 13.8 %all-to-all-start = ((s32[128,1,16]{2,1,0:T(1,128)}), s32[128,1,16]{2,1,0:T(1,128)S(1)}, u32[]{:S(2)}, u32[]{:S(2)}) async-start(s32[128,1,16]{2,1,0:T(1,128)} %copy.21), calls=%async_computation | async-start | bytes 131072 | tf_op jit(solution)/shard_map/all_to_all | solution.py:66
  38.3 2.6 scatter_custom_fusion.2
  41.1 2.1 all_gather.11
  43.3 5.6 %all-to-all-done = s32[128,1,16]{2,1,0:T(1,128)S(1)} async-done(((s32[128,1,16]{2,1,0:T(1,128)}), s32[128,1,16]{2,1,0:T(1,128)S(1)}, u32[]{:S(2)}, u32[]{:S(2)}) %all-to-all-start) | async-done | bytes 8224 | tf_op jit(solution)/shard_map/all_to_all | solution.py:66
  48.8 18.3 %all_to_all.35 = s32[128,1,16]{2,1,0:T(1,128)S(1)} all-to-all(s32[128,1,16]{2,1,0:T(1,128)S(1)} %copy.25), channel_id=1, replica_groups=mesh['mass'=128,'rep'=2] {'mass'}, dimensions={0} | all-to-all | bytes 16384 | tf_op jit(solution)/shard_map/all_to_all | solution.py:67
  67.2 7.6 %all-to-all-start.1 = ((bf16[128,16,1024]{2,1,0:T(8,128)(2,1)}), bf16[128,16,1024]{2,1,0:T(8,128)(2,1)}, u32[]{:S(2)}, u32[]{:S(2)}) async-start(bf16[128,16,1024]{2,1,0:T(8,128)(2,1)} %all-gather.2.cloned.1.call-done), calls=%async_computation.1 | async-start | bytes 8388608 | tf_op jit(solution)/shard_map/all_to_all | solution.py:65
  76.7 1.3 collective-permute-start
  78.6 0.8 reduce.15
  79.7 1.8 collective-permute-done
  81.5 85.8 %all-to-all-done.1 = bf16[128,16,1024]{2,1,0:T(8,128)(2,1)} async-done(((bf16[128,16,1024]{2,1,0:T(8,128)(2,1)}), bf16[128,16,1024]{2,1,0:T(8,128)(2,1)}, u32[]{:S(2)}, u32[]{:S(2)}) %all-to-all-start.1) | async-done | bytes 4194336 | tf_op jit(solution)/shard_map/all_to_all | solution.py:65
  167.3 3.4 %fusion.26 = bf16[256,1024]{1,0:T(8,128)(2,1)S(1)} fusion(bf16[2048,1024]{1,0:T(8,128)(2,1)} %bitcast.9, s32[2048]{0:T(1024)S(1)} %add_bitcast_fusion, pred[2048]{0:T(1024)(128)(4,1)S(1)} %ge.17), kind=kOutput, calls=%fused_computation.28 | convolution fusion | flops 1075052544 | bytes 4728832 | tf_op jit(solution)/shard_map/dot_general | solution.py:23
  170.8 1.3 collective-permute-start.1
  172.1 8.1 %select_reduce_fusion = f32[1024]{0:T(1024)S(1)} fusion(bf16[2048,1024]{1,0:T(8,128)(2,1)} %bitcast.9, s32[2048]{0:T(1024)S(1)} %eq.104, s32[1024]{0:T(1024)S(1)} %eq.99, bf16[128,2,8,1024]{3,2,1,0:T(8,128)(2,1)} %bitcast.7, s32[]{:T(128)S(6)} %select_n.33), kind=kOutput, calls=%fused_computation.4 | convolution fusion | flops 4307549184 | bytes 6307844 | tf_op jit(solution)/shard_map/dot_general | solution.py:32
  180.2 1.2 collective-permute-done.1
  181.4 2.5 select_reduce_fusion.2
  183.9 2.9 fusion.2
  187.0 7.8 %psum.15 = f32[64]{0:T(128)S(1)} all-reduce(f32[64]{0:T(128)S(1)} %convert_reduce_fusion), channel_id=1, replica_groups=mesh['mass'=128,'rep'=2] {'rep'}, use_global_device_ids=true, to_apply=%region_14.15 | all-reduce | flops 64 | bytes 512 | tf_op jit(solution)/shard_map/psum | solution.py:90
  194.7 27.3 %all-reduce.2.cloned.1.call-done = f32[64,1024]{1,0:T(8,128)} async-done(((f32[64,1024]{1,0:T(8,128)}), f32[64,1024]{1,0:T(8,128)}) %all-reduce.2.cloned.1.call-update) | async-done | bytes 262160 | tf_op jit(solution)/shard_map/psum | solution.py:90
  222.0 1.0 divide_convert_fusion
  223.0 2.1 convert_bitcast_fusion
  225.2 13.6 %all-to-all-start.3 = ((bf16[128,8,1024]{2,1,0:T(8,128)(2,1)}), bf16[128,8,1024]{2,1,0:T(8,128)(2,1)S(1)}, u32[]{:S(2)}, u32[]{:S(2)}) async-start(bf16[128,8,1024]{2,1,0:T(8,128)(2,1)} %convert_bitcast_fusion), calls=%async_computation.3 | async-start | bytes 4194304 | tf_op jit(solution)/shard_map/all_to_all | solution.py:99
  238.7 0.6 constant_dynamic-slice_fusion
  239.4 48.9 %all-to-all-done.3 = bf16[128,8,1024]{2,1,0:T(8,128)(2,1)S(1)} async-done(((bf16[128,8,1024]{2,1,0:T(8,128)(2,1)}), bf16[128,8,1024]{2,1,0:T(8,128)(2,1)S(1)}, u32[]{:S(2)}, u32[]{:S(2)}) %all-to-all-start.3) | async-done | bytes 2097184 | tf_op jit(solution)/shard_map/all_to_all | solution.py:99
  288.3 2.8 gather_fusion
  (40 shorter events, 3.7 us)
Async XLA Ops:
  7.2 60.0 %all-gather.2.cloned.1.call-start = ((), (), s32[]{:S(2)}) async-start(), calls=%async_computation.4 | async-start | bytes 6291456 | tf_op jit(solution)/shard_map/all_gather | solution.py:60
  24.6 24.3 %all-to-all-start = ((s32[128,1,16]{2,1,0:T(1,128)}), s32[128,1,16]{2,1,0:T(1,128)S(1)}, u32[]{:S(2)}, u32[]{:S(2)}) async-start(s32[128,1,16]{2,1,0:T(1,128)} %copy.21), calls=%async_computation | async-start | bytes 131072 | tf_op jit(solution)/shard_map/all_to_all | solution.py:66
  67.2 100.2 %all-to-all-start.1 = ((bf16[128,16,1024]{2,1,0:T(8,128)(2,1)}), bf16[128,16,1024]{2,1,0:T(8,128)(2,1)}, u32[]{:S(2)}, u32[]{:S(2)}) async-start(bf16[128,16,1024]{2,1,0:T(8,128)(2,1)} %all-gather.2.cloned.1.call-done), calls=%async_computation.1 | async-start | bytes 8388608 | tf_op jit(solution)/shard_map/all_to_all | solution.py:65
  74.7 147.3 %all-reduce.2.cloned.1.call-start = ((), (), s32[]{:S(2)}) async-start(), calls=%async_computation.5 | async-start | bytes 524288 | tf_op jit(solution)/shard_map/psum | solution.py:90
  76.7 4.8 %collective-permute-start = (s32[256]{0:T(256)S(1)}, s32[256]{0:T(256)S(1)}, u32[]{:S(2)}, u32[]{:S(2)}) collective-permute-start(s32[256]{0:T(256)S(1)} %select_reduce_fusion.1), channel_id=1, source_target_pairs={{2,0},{4,2},{6,4},{8,6},{10,8},{12,10},{14,12},{16,14},{18,16},{20... | collective-permute-start | bytes 3080 | tf_op jit(solution)/shard_map/ppermute | solution.py:16
  170.8 10.6 %collective-permute-start.1 = (bf16[256,1024]{1,0:T(8,128)(2,1)S(1)}, bf16[256,1024]{1,0:T(8,128)(2,1)S(1)}, u32[]{:S(2)}, u32[]{:S(2)}) collective-permute-start(bf16[256,1024]{1,0:T(8,128)(2,1)S(1)} %fusion.26), channel_id=1, source_target_pairs={{2,0},{4,2},{6,4},{8,6},{10,8},{12,10},{14,12},{16,14},{18,16},{20... | collective-permute-start | bytes 1572872 | tf_op jit(solution)/shard_map/ppermute | solution.py:16
  225.2 63.1 %all-to-all-start.3 = ((bf16[128,8,1024]{2,1,0:T(8,128)(2,1)}), bf16[128,8,1024]{2,1,0:T(8,128)(2,1)S(1)}, u32[]{:S(2)}, u32[]{:S(2)}) async-start(bf16[128,8,1024]{2,1,0:T(8,128)(2,1)} %convert_bitcast_fusion), calls=%async_computation.3 | async-start | bytes 4194304 | tf_op jit(solution)/shard_map/all_to_all | solution.py:99
Sparse Core Ops, SparseCore 0:
  16.5 23.5 all-gather.1
  187.0 35.0 all-reduce.1
where the time goes:
time: 300 us; the launch traced here: 298 us
  waiting for transfers between devices  171 us (57%)
  starting transfers between devices  37.6 us (13%)
  blocking collectives  32.9 us (11%)
  matrix products  19.1 us (6%)
  between operations  14.2 us (5%)
  local copies, waits for them, and re-layouts  11.8 us (4%)
  other arithmetic  11.7 us (4%)
    all_to_all x1, waiting for transfers between devices, body(): lax.all_to_all(pair_rows, 'mass', split_axis=0, concat_axis=0, tiled=True)  85.8 us
    all_to_all x1, waiting for transfers between devices, body(): lax.all_to_all(answers, 'mass', split_axis=0, concat_axis=0, tiled=True)  48.9 us
    psum x1, waiting for transfers between devices, body(): numerator, member_count = lax.psum((numerator, member_count), 'rep')  27.3 us
    all_to_all x1, blocking collectives, body(): lax.all_to_all(pair_edges, 'mass', split_axis=0, concat_axis=0, tiled=True)  18.3 us
    all_to_all x1, starting transfers between devices, body(): lax.all_to_all(pair_labels, 'mass', split_axis=0, concat_axis=0, tiled=True)  13.8 us
    all_to_all x1, starting transfers between devices, body(): lax.all_to_all(answers, 'mass', split_axis=0, concat_axis=0, tiled=True)  13.6 us
    dot_general x2, matrix products, density_of(): lax.dot_general(query_rows, cand_rows, (((1,), (1,)), ((), ())), preferre...  10.6 us
    psum x1, blocking collectives, body(): numerator, member_count = lax.psum((numerator, member_count), 'rep')  7.78 us
  transfers between devices with their start and end apart: 7, of which 6 were waited for; matrix products, arithmetic and copies ran while one was open for 6% of the time, Pallas kernels for 0%

commit v1 on v0

v1 whole, which is shorter than its diff:
```python
import functools

import jax
import jax.numpy as jnp
from jax import lax
from jax.experimental import pallas as pl
from jax.experimental.pallas import tpu as pltpu
from jax.sharding import PartitionSpec as P

MESH = pl.DeviceIdType.MESH
CLUSTERS = 64
SLOTS = 8
BETA = 6.0
F32 = jnp.float32
BF16 = jnp.bfloat16
NT = (((1,), (1,)), ((), ()))


def iota(shape, dim):
    return lax.broadcasted_iota(jnp.int32, shape, dim)


def onehot(cond):
    return jnp.where(cond, 1.0, 0.0).astype(BF16)


def mm(a, b):
    return jnp.dot(a, b, preferred_element_type=F32)


def mm_nt(a, b):
    return lax.dot_general(a, b, NT, preferred_element_type=F32)


def kernel(
    x_ref, code_ref, cons_ref, out_ref,
    unit, send, msend, own, sib, mown, msib, edge_send, edge_own, edge_sib, medge, num, num_sib, cnt, cnt_sib,
    table, ret, acc, dens, lab_col,
    send_sem, msend_sem, ret_send_sem, row_sem, meta_sem, ret_sem, pair_send, pair_recv, edge_ssem, edge_rsem, loc_sem,
):
    me = lax.axis_index("mass")
    rep = lax.axis_index("rep")
    other = 1 - rep
    n = 128
    x, z, y = me // 32, (me // 4) % 8, me % 4
    prev = lax.rem(me + n - 1, n)

    def target(d):
        dx, dz, dy = d // 32, (d // 4) % 8, d % 4
        return lax.rem(x + dx, 4) * 32 + lax.rem(z + dz, 8) * 4 + lax.rem(y + dy, 4)

    barrier = pltpu.get_barrier_semaphore()

    @pl.loop(1, n)
    def _(d):
        pl.semaphore_signal(barrier, inc=1, device_id=(target(d), rep), device_id_type=MESH)

    pl.semaphore_signal(barrier, inc=1, device_id=(me, other), device_id_type=MESH)

    wide = x_ref[...].astype(F32)
    unit[...] = (wide * lax.rsqrt(jnp.mean(wide * wide, axis=1, keepdims=True) + 1e-6)).astype(BF16)

    code_row = code_ref[...]
    rows = code_row.shape[1]
    diag = iota((rows, rows), 0) == iota((rows, rows), 1)
    code_col = jnp.sum(jnp.where(diag, code_row.astype(F32), 0.0), axis=1, keepdims=True).astype(jnp.int32)

    def fields(code):
        return code >> 13, (code >> 7) & 63, code & 127

    w_row, _, e_row = fields(code_row)
    w_col, l_col, e_col = fields(code_col)
    key_row = iota((1, rows), 1) - jnp.where(e_row > 0, rows, 0)
    key_col = iota((rows, 1), 0) - jnp.where(e_col > 0, rows, 0)
    same = w_col == w_row
    rank_row = jnp.sum(jnp.where(same & (key_col < key_row), 1.0, 0.0), axis=0, keepdims=True).astype(jnp.int32)
    rank_col = jnp.sum(jnp.where(same & (key_row < key_col), 1.0, 0.0), axis=1, keepdims=True).astype(jnp.int32)
    slot_row = w_row * SLOTS + rank_row
    slot_col = w_col * SLOTS + rank_col

    for c in range(4):
        pick = onehot(iota((256, rows), 0) + 256 * c == slot_row)
        send[pl.ds(32 * c, 32)] = mm(pick, unit[...]).reshape(32, SLOTS, 1024).astype(BF16)

    lane = iota((rows, 128), 1)
    code2 = jnp.where(lane == rank_col, l_col + 1, 0) + jnp.where(lane == rank_col + SLOTS, e_col, 0)
    meta = mm(onehot(iota((n, rows), 0) == w_row), code2.astype(F32).astype(BF16))
    msend[...] = meta.reshape(n, 1, 128)

    pl.semaphore_wait(barrier, n)

    def row_copy(t, s):
        return pltpu.make_async_remote_copy(
            src_ref=send.at[t], dst_ref=own.at[s], send_sem=send_sem, recv_sem=row_sem.at[s // 32],
            device_id=(t, rep), device_id_type=MESH)

    def meta_copy(t, s):
        return pltpu.make_async_remote_copy(
            src_ref=msend.at[t], dst_ref=mown.at[s], send_sem=msend_sem, recv_sem=meta_sem,
            device_id=(t, rep), device_id_type=MESH)

    pltpu.make_async_copy(send.at[me], own.at[me], row_sem.at[x]).start()
    pltpu.make_async_copy(msend.at[me], mown.at[me], meta_sem).start()

    @pl.loop(1, n)
    def _(d):
        t = target(d)
        row_copy(t, me).start()
        meta_copy(t, me).start()

    def pair_copy(src, dst, k):
        return pltpu.make_async_remote_copy(
            src_ref=src, dst_ref=dst, send_sem=pair_send.at[k], recv_sem=pair_recv.at[k],
            device_id=(me, other), device_id_type=MESH)

    pair_copies = []
    for q in range(4):
        s = lax.rem(x + 4 - q, 4)
        part = pl.ds(s * 32, 32)
        pltpu.make_async_copy(send.at[part], own.at[part], row_sem.at[s]).wait()
        copy = pair_copy(own.at[part], sib.at[part], q)
        copy.start()
        pair_copies.append(copy)
    pltpu.make_async_copy(msend, mown, meta_sem).wait()
    copy = pair_copy(mown, msib, 4)
    copy.start()
    pair_copies.append(copy)

    first = onehot(iota((n, n * SLOTS), 1) == SLOTS * iota((n, n * SLOTS), 0))
    own_rows = own[...].reshape(n * SLOTS, 1024)
    edge_send[...] = mm(first, own_rows).astype(BF16)
    edge_copies = [
        pltpu.make_async_remote_copy(
            src_ref=src, dst_ref=dst, send_sem=edge_ssem.at[k], recv_sem=edge_rsem.at[k],
            device_id=(prev, rep), device_id_type=MESH)
        for k, (src, dst) in enumerate([(edge_send, edge_own), (mown, medge.at[0])])
    ]
    for copy in edge_copies:
        copy.start()

    spread = onehot(iota((n * SLOTS, n), 0) // SLOTS == iota((n * SLOTS, n), 1))
    slot_lane = iota((n * SLOTS, n), 1) == iota((n * SLOTS, n), 0) % SLOTS

    def label_forms(meta_in):
        per_slot = jnp.where(slot_lane, mm(spread, meta_in.astype(BF16)), 0.0)
        col = jnp.sum(per_slot, axis=1, keepdims=True)
        row = mm_nt(jnp.ones((8, n), BF16), per_slot.astype(BF16))[0:1]
        return col, row

    col, row_own = label_forms(mown[...].reshape(n, 128))
    lab_col[...] = col

    def add_density(cand, cand_labels, begin):
        for q in range(4):
            part = pl.ds(q * 256, 256)
            scores = mm_nt(own[pl.ds(q * 32, 32)].reshape(256, 1024), cand) * (1.0 / 1024.0)
            kept = jnp.where(lab_col[part] == cand_labels, jnp.exp(BETA * (scores - 1.0)), 0.0)
            total = jnp.sum(kept, axis=1, keepdims=True)
            dens[part] = total if begin else dens[part] + total

    add_density(own_rows, row_own, True)
    for copy in pair_copies:
        copy.wait()
    _, row_sib = label_forms(msib[...].reshape(n, 128))
    for copy in edge_copies:
        copy.wait()
    relay = [pair_copy(edge_own, edge_sib, 5), pair_copy(medge.at[0], medge.at[1], 6)]
    for copy in relay:
        copy.start()
    add_density(sib[...].reshape(n * SLOTS, 1024), row_sib, False)
    edge_lane = onehot(iota((8, 128), 1) == SLOTS)
    live = me < n - 1

    def edge_labels(k):
        codes = mm_nt(edge_lane, medge[k].reshape(n, 128).astype(BF16))[0:1]
        return jnp.where(live, codes, 0.0)

    for copy in relay:
        copy.wait()
    add_density(
        jnp.concatenate([edge_own[...], edge_sib[...]], axis=0),
        jnp.concatenate([edge_labels(0), edge_labels(1)], axis=1), False)

    weighted = (dens[...] * own_rows.astype(F32)).astype(BF16)
    member = onehot(iota((CLUSTERS, n * SLOTS), 0) + 1 == row_own.astype(jnp.int32))
    num[...] = mm(member, weighted)
    cnt[...] = jnp.broadcast_to(jnp.sum(member.astype(F32), axis=1, keepdims=True), (CLUSTERS, 128))
    pair_num = [pair_copy(num, num_sib, 7), pair_copy(cnt, cnt_sib, 8)]
    for copy in pair_num:
        copy.start()
    for copy in pair_num:
        copy.wait()
    table[...] = ((num[...] + num_sib[...]) / (cnt[:, 0:1] + cnt_sib[:, 0:1] + 1.0)).astype(BF16)
    cons_ref[...] = table[:, pl.ds(pl.multiple_of(rep * 512, 512), 512)]

    pltpu.make_async_remote_copy(
        src_ref=send.at[pl.ds(0, n - 1)], dst_ref=own.at[pl.ds(0, n - 1)], send_sem=send_sem, recv_sem=row_sem.at[0],
        device_id=(me, other), device_id_type=MESH).wait_send()
    pltpu.make_async_remote_copy(
        src_ref=msend.at[pl.ds(0, n - 1)], dst_ref=mown.at[pl.ds(0, n - 1)], send_sem=msend_sem, recv_sem=meta_sem,
        device_id=(me, other), device_id_type=MESH).wait_send()

    def ret_copy(t, s):
        return pltpu.make_async_remote_copy(
            src_ref=send.at[t], dst_ref=ret.at[s], send_sem=ret_send_sem, recv_sem=ret_sem.at[s // 32],
            device_id=(t, rep), device_id_type=MESH)

    for q in range(4):
        qx = lax.rem(x + q, 4)
        part = pl.ds(pl.multiple_of(qx * 256, 256), 256)
        pick = onehot(iota((256, CLUSTERS), 1) + 1 == lab_col[part].astype(jnp.int32))
        send[pl.ds(qx * 32, 32)] = mm(pick, table[...]).reshape(32, SLOTS, 1024).astype(BF16)
        if q == 0:
            pltpu.make_async_copy(send.at[me], ret.at[me], ret_sem.at[x]).start()

        @pl.loop(max(1, 32 * q), 32 * q + 32)
        def _(d):
            ret_copy(target(d), me).start()

    for q in range(4):
        s = lax.rem(x + 4 - q, 4)
        part = pl.ds(s * 32, 32)
        pltpu.make_async_copy(send.at[part], ret.at[part], ret_sem.at[s]).wait()
        pick = onehot(iota((rows, 256), 1) + 256 * s == slot_col)
        got = mm(pick, ret[part].reshape(256, 1024))
        if q == 0:
            acc[...] = got
        elif q < 3:
            acc[...] += got
        else:
            out_ref[...] = (acc[...] + got).astype(BF16)
    pltpu.make_async_remote_copy(
        src_ref=send.at[pl.ds(0, n - 1)], dst_ref=ret.at[pl.ds(0, n - 1)], send_sem=ret_send_sem, recv_sem=ret_sem.at[0],
        device_id=(me, other), device_id_type=MESH).wait_send()


def body(spectra, window, labels, edge_labels):
    rows, dim = spectra.shape
    n = lax.axis_size("mass")
    code = (window * 8192 + labels * 128 + edge_labels + 1).reshape(1, rows)
    vm = lambda shape, t=BF16: pltpu.VMEM(shape, t)
    block = (n, SLOTS, dim)
    meta = (n, 1, 128)
    dma = pltpu.SemaphoreType.DMA
    return pl.pallas_call(
        kernel,
        out_shape=(
            jax.ShapeDtypeStruct((CLUSTERS, dim // 2), BF16),
            jax.ShapeDtypeStruct((rows, dim), BF16),
        ),
        in_specs=[pl.BlockSpec(memory_space=pltpu.VMEM)] * 2,
        out_specs=(pl.BlockSpec(memory_space=pltpu.VMEM), pl.BlockSpec(memory_space=pltpu.VMEM)),
        scratch_shapes=[
            vm((rows, dim)), vm(block), vm(meta, F32), vm(block), vm(block), vm(meta, F32), vm(meta, F32),
            vm((n, dim)), vm((n, dim)), vm((n, dim)), vm((2,) + meta, F32),
            vm((CLUSTERS, dim), F32), vm((CLUSTERS, dim), F32), vm((CLUSTERS, 128), F32), vm((CLUSTERS, 128), F32),
            vm((CLUSTERS, dim)), vm(block), vm((rows, dim), F32), vm((n * SLOTS, 1), F32), vm((n * SLOTS, 1), F32),
            dma, dma, dma, dma((4,)), dma, dma((4,)), dma((9,)), dma((9,)), dma((2,)), dma((2,)), dma,
        ],
        compiler_params=pltpu.CompilerParams(
            collective_id=0, has_side_effects=True, vmem_limit_bytes=56 * 1024 * 1024),
        cost_estimate=pl.CostEstimate(flops=8 * 10**9, bytes_accessed=4 * 10**6, transcendentals=2 * 10**6),
        name="consensus",
    )(spectra, code)


def solution(mesh):
    placed = (P(("mass", "rep"), None), P(("mass", "rep")), P(("mass", "rep")), P(("mass", "rep")))
    return jax.shard_map(
        body,
        mesh=mesh,
        in_specs=placed,
        out_specs=(P("mass", "rep"), P(("mass", "rep"), None)),
        check_vma=False,
    )
```

time: 300 us -> 141 us (0.47)
  waiting for transfers between devices: 171 us -> 0 us
  Pallas kernels: 0 us -> 135 us
  starting transfers between devices: 37.6 us -> 0 us
  blocking collectives: 32.9 us -> 0 us
  matrix products: 19.1 us -> 0 us
  between operations: 14.2 us -> 0.64 us
  other arithmetic: 11.7 us -> 1.3 us
  local copies, waits for them, and re-layouts: 11.8 us -> 3.74 us
    all_to_all x3 -> x0, waiting for transfers between devices: 140 us -> none  [the longest x1 85.8 us: body(): lax.all_to_all(pair_rows, 'mass', split_axis=0, concat_axis=0, tiled=True)]
    pallas_call x0 -> x1, Pallas kernels: none -> 135 us  [body(): pl.pallas_call(kernel, out_shape=(jax.ShapeDtypeStruct((CLUSTERS, dim //...]
    all_to_all x3 -> x0, starting transfers between devices: 34.9 us -> none  [the longest x1 13.8 us: body(): lax.all_to_all(pair_labels, 'mass', split_axis=0, concat_axis=0, tiled=True)]
    psum x1 -> x0, waiting for transfers between devices: 27.3 us -> none  [body(): numerator, member_count = lax.psum((numerator, member_count), 'rep')]
    dot_general x5 -> x0, matrix products: 19.1 us -> none  [the longest x2 10.6 us: density_of(): lax.dot_general(query_rows, cand_rows, (((1,), (1,)), ((), ())), preferre...]
    all_to_all x1 -> x0, blocking collectives: 18.3 us -> none  [body(): lax.all_to_all(pair_edges, 'mass', split_axis=0, concat_axis=0, tiled=True)]
    psum x1 -> x0, blocking collectives: 7.78 us -> none  [body(): numerator, member_count = lax.psum((numerator, member_count), 'rep')]
    all_gather x2 -> x0, blocking collectives: 6.83 us -> none  [the longest x1 4.74 us: body(): lax.all_gather(send_labels.reshape(windows, capacity), 'rep', axis=1, til...]
  transfers between devices with their start and end apart: 7 -> 0, of which waited for: 6 -> 0; matrix products, arithmetic and copies ran while one was open for 6% -> 0% of each run, Pallas kernels for 0% -> 0%
where the time goes in v1:
time: 141 us
  Pallas kernels  135 us (96%)
  local copies, waits for them, and re-layouts  3.74 us (3%)
    pallas_call x1, Pallas kernels, body(): pl.pallas_call(kernel, out_shape=(jax.ShapeDtypeStruct((CLUSTERS, dim //...  135 us
    unnamed x2, local copies, waits for them, and re-layouts  3.74 us

profile of v1, /device:TPU:1, one launch (start us, length us, event | category | flops | bytes accessed | tf_op | source)
XLA Modules:
  0.0 140.5 jit_solution(10037637733060546262)
XLA Ops:
  0.6 1.3 add_add_fusion
  1.9 134.9 %consensus.1 = (bf16[64,512]{1,0:T(8,128)(2,1)}, bf16[512,1024]{1,0:T(8,128)(2,1)}) custom-call(bf16[512,1024]{1,0:T(8,128)(2,1)} %x_ref.1, s32[1,512]{1,0:T(1,128)} %bitcast.1), custom_call_target="tpu_custom_call" | custom-call | flops 8000000000 | bytes 4000000 | tf_op jit(solution)/shard_map/consensus/pallas_call | solution.py:245
  136.8 1.5 %copy.8 = bf16[64,512]{1,0:T(8,128)(2,1)} copy(bf16[64,512]{1,0:T(8,128)(2,1)} %get-tuple-element.4) | data formatting | bytes 131072
  138.3 2.3 %copy.9 = bf16[512,1024]{1,0:T(8,128)(2,1)} copy(bf16[512,1024]{1,0:T(8,128)(2,1)} %get-tuple-element.5) | data formatting | bytes 2097152

commit v2 on v1

v2 whole, which is shorter than its diff:
```python
import functools

import jax
import jax.numpy as jnp
from jax import lax
from jax.experimental import pallas as pl
from jax.experimental.pallas import tpu as pltpu
from jax.sharding import PartitionSpec as P

MESH = pl.DeviceIdType.MESH
CLUSTERS = 64
SLOTS = 8
BETA = 6.0
F32 = jnp.float32
BF16 = jnp.bfloat16
NT = (((1,), (1,)), ((), ()))


def iota(shape, dim):
    return lax.broadcasted_iota(jnp.int32, shape, dim)


def onehot(cond):
    return jnp.where(cond, 1.0, 0.0).astype(BF16)


def mm(a, b):
    return jnp.dot(a, b, preferred_element_type=F32)


def mm_nt(a, b):
    return lax.dot_general(a, b, NT, preferred_element_type=F32)


ZO = (0, 1, 7, 2, 6, 3, 5, 4)
GROUPS = ((0, 32), (32, 32), (64, 32), (96, 16), (112, 16))


def depth_of(j):
    return jnp.where(j % 2 == 1, (j + 1) // 2, (8 - j // 2) % 8)


def order_of(depth):
    return jnp.where(depth > 4, 2 * (8 - depth), jnp.maximum(2 * depth - 1, 0))


def kernel(
    x_ref, code_ref, cons_ref, out_ref,
    unit, send, own, sib, ret, acc, msend, mplane, mz, mz_sib, ztab,
    edge_send, edge_own, edge_sib, ecode_send, ecode_own, ecode_sib, num, num_sib, cnt, cnt_sib, dens, lab_col,
    line_a, line_b, row_ssem, row_sem, ret_ssem, ret_sem, mp_ssem, mp_sem, mz_ssem, mz_sem,
    pair_ssem, pair_sem, edge_ssem, edge_sem, zt_ssem, zt_sem, zp_ssem, zp_sem,
):
    me = lax.axis_index("mass")
    rep = lax.axis_index("rep")
    other = 1 - rep
    n = 128
    rows = x_ref.shape[0]
    x, z, y = me // 32, (me // 4) % 8, me % 4

    def chip(dx, dz, dy):
        return ((x + dx) % 4) * 32 + ((z + dz) % 8) * 4 + (y + dy) % 4

    def signal(sem, m, r):
        pl.semaphore_signal(sem, inc=1, device_id=(m, r), device_id_type=MESH)

    def remote(src, dst, ssem, rsem, m, r):
        return pltpu.make_async_remote_copy(
            src_ref=src, dst_ref=dst, send_sem=ssem, recv_sem=rsem, device_id=(m, r), device_id_type=MESH)

    barrier = pltpu.get_barrier_semaphore()
    for k in range(1, 8):
        signal(barrier, chip(0, k, 0), rep)
    for k in range(1, 4):
        signal(barrier, chip(k, 0, 0), rep)
        signal(barrier, chip(0, 0, k), rep)
    signal(barrier, me, other)

    code_row = code_ref[...]
    diag = iota((rows, rows), 0) == iota((rows, rows), 1)
    code_col = jnp.sum(jnp.where(diag, code_row.astype(F32), 0.0), axis=1, keepdims=True).astype(jnp.int32)

    def fields(code):
        return code >> 13, (code >> 7) & 63, code & 127

    w_row, _, e_row = fields(code_row)
    w_col, l_col, e_col = fields(code_col)
    key_row = iota((1, rows), 1) - jnp.where(e_row > 0, rows, 0)
    key_col = iota((rows, 1), 0) - jnp.where(e_col > 0, rows, 0)
    same = w_col == w_row
    rank_row = jnp.sum(jnp.where(same & (key_col < key_row), 1.0, 0.0), axis=0, keepdims=True).astype(jnp.int32)
    rank_col = jnp.sum(jnp.where(same & (key_row < key_col), 1.0, 0.0), axis=1, keepdims=True).astype(jnp.int32)

    def place(window):
        plane = (((window >> 5) - x) & 3) * 4 + ((window - y) & 3)
        return plane, order_of(((window >> 2) - z) & 7)

    plane_row, order_row = place(w_row)
    plane_col, order_col = place(w_col)
    slot_row = (plane_row * 8 + order_row) * SLOTS + rank_row
    slot_col = (order_col * 16 + plane_col) * SLOTS + rank_col

    pl.semaphore_wait(barrier, 14)
    for k in range(1, 4):
        signal(line_a, chip(0, 0, k), rep)

    wide = x_ref[...].astype(F32)
    unit[...] = (wide * lax.rsqrt(jnp.mean(wide * wide, axis=1, keepdims=True) + 1e-6)).astype(BF16)

    pl.semaphore_wait(line_a, 3)
    for k in range(1, 4):
        signal(line_b, chip(k, 0, 0), rep)

    lane = iota((rows, 128), 1) - ((w_col >> 2) & 7) * 16
    code2 = jnp.where(lane == rank_col, l_col + 1, 0) + jnp.where(lane == rank_col + SLOTS, e_col, 0)
    meta = mm(onehot(iota((16, rows), 0) == plane_row), code2.astype(F32).astype(BF16))
    msend[...] = meta.reshape(16, 1, 128)

    def pack(c):
        pick = onehot(iota((256, rows), 0) + 256 * c == slot_row)
        send[pl.ds(32 * c, 32)] = mm(pick, unit[...]).reshape(32, SLOTS, 1024).astype(BF16)

    pack(0)
    pl.semaphore_wait(line_b, 3)

    def plane_copy(p, sign):
        return remote(msend.at[p], mplane.at[p], mp_ssem, mp_sem, chip(sign * (p // 4), 0, sign * (p % 4)), rep)

    pltpu.make_async_copy(msend.at[0], mplane.at[0], mp_sem).start()
    pltpu.make_async_copy(send.at[0], own.at[0], row_sem.at[0]).start()
    for p in range(1, 16):
        plane_copy(p, 1).start()

    def send_rows(group):
        begin, count = GROUPS[group]

        @pl.loop(max(1, begin), begin + count)
        def _(d):
            p = d // 8
            m = chip(p // 4, depth_of(d % 8), p % 4)
            remote(send.at[d], own.at[d], row_ssem, row_sem.at[group], m, rep).start()

    send_rows(0)
    for c in range(1, 4):
        pack(c)
    send_rows(1)

    pltpu.make_async_copy(msend, mplane, mp_sem).wait()
    mz[0] = mplane[...].reshape(16, 128).astype(BF16)
    for j in range(1, 8):
        remote(mz.at[0], mz.at[j], mz_ssem.at[j], mz_sem.at[j], chip(0, ZO[j], 0), rep).start()
    send_rows(2)
    send_rows(3)
    send_rows(4)

    def pair(src, dst, k):
        return remote(src, dst, pair_ssem.at[k], pair_sem.at[k], me, other)

    for j in range(1, 8):
        remote(mz.at[0], mz.at[j], mz_ssem.at[j], mz_sem.at[j], chip(0, ZO[j], 0), rep).wait()
    pair_meta = pair(mz, mz_sib, 5)
    pair_meta.start()

    slot_i = iota((n * SLOTS, n), 0)
    slot_c = iota((n * SLOTS, n), 1)
    spread = onehot(slot_c == ((slot_i >> 3) & 7) * 16 + (slot_i >> 6))
    slot_lane = slot_c == (slot_i & 7) + z * 16
    ones = jnp.ones((8, n), BF16)

    def label_forms(codes):
        every = mm(spread, codes)
        per_slot = jnp.where(slot_lane, every, 0.0)
        return every, jnp.sum(per_slot, axis=1, keepdims=True), mm_nt(ones, per_slot.astype(BF16))[0:1]

    _, col, row_own = label_forms(mz[...].reshape(n, 128))
    lab_col[...] = col
    block_i = iota((n, n), 0)
    blocks = mm(onehot(iota((n, n), 1) == (block_i & 7) * 16 + (block_i >> 3)), mz[...].reshape(n, 128))
    ecode = jnp.sum(jnp.where(iota((n, n), 1) == z * 16 + SLOTS, blocks, 0.0), axis=1, keepdims=True)
    ecode_send[...] = jnp.broadcast_to(ecode, (n, 128)).astype(BF16)
    below = (me + n - 1) % n
    edge_code_copy = remote(ecode_send, ecode_own, edge_ssem.at[5], edge_sem.at[5], below, rep)
    edge_code_copy.start()
    pair_meta.wait()
    _, _, row_sib = label_forms(mz_sib[...].reshape(n, 128))
    dens[...] = jnp.zeros((n * SLOTS, 1), F32)

    def flat(ref, begin, end):
        return ref[pl.ds(begin, end - begin)].reshape((end - begin) * SLOTS, 1024)

    def add_density(begin, end, cand, cand_labels):
        for b in range(begin, end, 32):
            e = min(b + 32, end)
            part = pl.ds(b * SLOTS, (e - b) * SLOTS)
            scores = mm_nt(flat(own, b, e), cand) * (1.0 / 1024.0)
            kept = jnp.where(lab_col[part] == cand_labels, jnp.exp(BETA * (scores - 1.0)), 0.0)
            dens[part] += jnp.sum(kept, axis=1, keepdims=True)

    def group_pair(g):
        begin, count = GROUPS[g]
        part = pl.ds(begin, count)
        return pair(own.at[part], sib.at[part], g)

    def group_edge(g):
        begin, count = GROUPS[g]
        part = pl.ds(begin, count)
        return remote(edge_send.at[part], edge_own.at[part], edge_ssem.at[g], edge_sem.at[g], below, rep)

    def arrive(g):
        begin, count = GROUPS[g]
        part = pl.ds(begin, count)
        pltpu.make_async_copy(send.at[part], own.at[part], row_sem.at[g]).wait()
        group_pair(g).start()
        first = onehot(iota((count, count * SLOTS), 1) == SLOTS * iota((count, count * SLOTS), 0))
        edge_send[part] = mm(first, flat(own, begin, begin + count)).astype(BF16)
        group_edge(g).start()

    def process(g):
        begin, count = GROUPS[g]
        end = begin + count
        new = slice(begin * SLOTS, end * SLOTS)
        seen = slice(0, end * SLOTS)
        add_density(begin, end, flat(own, 0, end), row_own[:, seen])
        if begin:
            add_density(0, begin, flat(own, begin, end), row_own[:, new])
        group_pair(g).wait()
        add_density(begin, end, flat(sib, 0, end), row_sib[:, seen])
        if begin:
            add_density(0, begin, flat(sib, begin, end), row_sib[:, new])

    for g in range(len(GROUPS)):
        arrive(g)
        if g:
            process(g - 1)
    for g in range(len(GROUPS)):
        group_edge(g).wait()
    edge_code_copy.wait()
    relay = [pair(edge_own, edge_sib, 6), pair(ecode_own, ecode_sib, 7)]
    for copy in relay:
        copy.start()
    process(len(GROUPS) - 1)
    for copy in relay:
        copy.wait()
    live = me < n - 1

    def edge_labels(ref):
        return jnp.where(live, mm_nt(onehot(iota((8, 128), 1) == 0), ref[...])[0:1], 0.0)

    add_density(0, n, edge_own[...], edge_labels(ecode_own))
    add_density(0, n, edge_sib[...], edge_labels(ecode_sib))

    weighted = (dens[...] * flat(own, 0, n).astype(F32)).astype(BF16)
    member = onehot(iota((CLUSTERS, n * SLOTS), 0) + 1 == row_own.astype(jnp.int32))
    num[...] = mm(member, weighted)
    cnt[...] = jnp.broadcast_to(jnp.sum(member.astype(F32), axis=1, keepdims=True), (CLUSTERS, 128))
    pair_num = [pair(num, num_sib, 8), pair(cnt, cnt_sib, 9)]
    for copy in pair_num:
        copy.start()
    remote(send.at[pl.ds(0, n - 1)], own.at[pl.ds(0, n - 1)], row_ssem, row_sem.at[0], me, other).wait_send()
    remote(msend.at[pl.ds(0, 15)], mplane.at[pl.ds(0, 15)], mp_ssem, mp_sem, me, other).wait_send()
    for copy in pair_num:
        copy.wait()
    ztab[0] = ((num[...] + num_sib[...]) / (cnt[:, 0:1] + cnt_sib[:, 0:1] + 1.0)).astype(BF16)

    half = pl.ds(pl.multiple_of(rep * 32, 32), 32)

    def table_copy(j):
        return remote(ztab.at[0, half], ztab.at[j, half], zt_ssem.at[j], zt_sem.at[j], chip(0, -ZO[j], 0), rep)

    def table_pair(j):
        return remote(ztab.at[j, half], ztab.at[j, half], zp_ssem.at[j], zp_sem.at[j], me, other)

    for j in range(1, 8):
        table_copy(j).start()
    cons_ref[...] = ztab[0, :, pl.ds(pl.multiple_of(rep * 512, 512), 512)]

    plane_i = iota((16 * SLOTS, 128), 0)
    plane_c = iota((16 * SLOTS, 128), 1)
    codes = mm(onehot(iota((16 * SLOTS, 16), 1) == plane_i[:, 0:16] >> 3), mz[0])

    def answer(j):
        at = ((z + ZO[j]) % 8) * 16
        labels = jnp.sum(jnp.where(plane_c == (plane_i & 7) + at, codes, 0.0), axis=1, keepdims=True)
        pick = onehot(iota((16 * SLOTS, CLUSTERS), 1) + 1 == labels.astype(jnp.int32))
        send[pl.ds(16 * j, 16)] = mm(pick, ztab[j]).reshape(16, SLOTS, 1024).astype(BF16)
        pltpu.make_async_copy(send.at[16 * j], ret.at[16 * j], ret_sem.at[j // 2]).start()

        @pl.loop(1, 16)
        def _(p):
            remote(send.at[16 * j + p], ret.at[16 * j + p], ret_ssem, ret_sem.at[j // 2],
                   chip(-(p // 4), 0, -(p % 4)), rep).start()

    for j in range(8):
        if j < 7:
            table_copy(j + 1).wait_recv()
            table_pair(j + 1).start()
        if j:
            table_pair(j).wait_recv()
        answer(j)

    for q in range(4):
        part = pl.ds(32 * q, 32)
        pltpu.make_async_copy(send.at[part], ret.at[part], ret_sem.at[q]).wait()
        pick = onehot(iota((rows, 256), 1) + 256 * q == slot_col)
        got = mm(pick, ret[part].reshape(256, 1024))
        if q == 0:
            acc[...] = got
        elif q < 3:
            acc[...] += got
        else:
            out_ref[...] = (acc[...] + got).astype(BF16)
    for j in range(1, 8):
        table_copy(j).wait_send()
        table_pair(j).wait_send()
    remote(send.at[pl.ds(0, 120)], ret.at[pl.ds(0, 120)], ret_ssem, ret_sem.at[0], me, other).wait_send()


def body(spectra, window, labels, edge_labels):
    rows, dim = spectra.shape
    n = lax.axis_size("mass")
    code = (window * 8192 + labels * 128 + edge_labels + 1).reshape(1, rows)
    vm = lambda shape, t=BF16: pltpu.VMEM(shape, t)
    block = (n, SLOTS, dim)
    dma = pltpu.SemaphoreType.DMA
    regular = pltpu.SemaphoreType.REGULAR
    return pl.pallas_call(
        kernel,
        out_shape=(
            jax.ShapeDtypeStruct((CLUSTERS, dim // 2), BF16),
            jax.ShapeDtypeStruct((rows, dim), BF16),
        ),
        in_specs=[pl.BlockSpec(memory_space=pltpu.VMEM)] * 2,
        out_specs=(pl.BlockSpec(memory_space=pltpu.VMEM), pl.BlockSpec(memory_space=pltpu.VMEM)),
        scratch_shapes=[
            vm((rows, dim)), vm(block), vm(block), vm(block), vm(block), vm((rows, dim), F32),
            vm((16, 1, 128), F32), vm((16, 1, 128), F32), vm((8, 16, 128)), vm((8, 16, 128)), vm((8, CLUSTERS, dim)),
            vm((n, dim)), vm((n, dim)), vm((n, dim)), vm((n, 128)), vm((n, 128)), vm((n, 128)),
            vm((CLUSTERS, dim), F32), vm((CLUSTERS, dim), F32), vm((CLUSTERS, 128), F32), vm((CLUSTERS, 128), F32),
            vm((n * SLOTS, 1), F32), vm((n * SLOTS, 1), F32),
            regular, regular, dma, dma((5,)), dma, dma((4,)), dma, dma, dma((8,)), dma((8,)),
            dma((10,)), dma((10,)), dma((6,)), dma((6,)), dma((8,)), dma((8,)), dma((8,)), dma((8,)),
        ],
        compiler_params=pltpu.CompilerParams(
            collective_id=0, has_side_effects=True, vmem_limit_bytes=56 * 1024 * 1024),
        cost_estimate=pl.CostEstimate(flops=8 * 10**9, bytes_accessed=4 * 10**6, transcendentals=2 * 10**6),
        name="consensus",
    )(spectra, code)


def solution(mesh):
    placed = (P(("mass", "rep"), None), P(("mass", "rep")), P(("mass", "rep")), P(("mass", "rep")))
    return jax.shard_map(
        body,
        mesh=mesh,
        in_specs=placed,
        out_specs=(P("mass", "rep"), P(("mass", "rep"), None)),
        check_vma=False,
    )
```

time: 141 us -> 115 us (0.82)
  Pallas kernels: 135 us -> 109 us
    pallas_call x1, Pallas kernels: 135 us -> 109 us  [body(): pl.pallas_call(kernel, out_shape=(jax.ShapeDtypeStruct((CLUSTERS, dim //...]
where the time goes in v2:
time: 115 us
  Pallas kernels  109 us (95%)
  local copies, waits for them, and re-layouts  3.74 us (3%)
  other arithmetic  1.3 us (1%)
    pallas_call x1, Pallas kernels, body(): pl.pallas_call(kernel, out_shape=(jax.ShapeDtypeStruct((CLUSTERS, dim //...  109 us
    unnamed x2, local copies, waits for them, and re-layouts  3.74 us

profile of v2, /device:TPU:1, one launch (start us, length us, event | category | flops | bytes accessed | tf_op | source)
XLA Modules:
  0.0 114.6 jit_solution(12079153404199225413)
XLA Ops:
  0.6 1.3 %add_add_fusion = s32[512]{0:T(512)} fusion(s32[512]{0:T(512)} %param.7, s32[512]{0:T(512)} %param.6, s32[512]{0:T(512)} %param.5), kind=kLoop, calls=%fused_computation | loop fusion | flops 2560 | bytes 8192 | tf_op jit(solution)/shard_map/add | solution.py:321
  1.9 108.9 %consensus.1 = (bf16[64,512]{1,0:T(8,128)(2,1)}, bf16[512,1024]{1,0:T(8,128)(2,1)}) custom-call(bf16[512,1024]{1,0:T(8,128)(2,1)} %x_ref.1, s32[1,512]{1,0:T(1,128)} %bitcast.1), custom_call_target="tpu_custom_call" | custom-call | flops 8000000000 | bytes 4000000 | tf_op jit(solution)/shard_map/consensus/pallas_call | solution.py:326
  110.8 1.5 %copy.8 = bf16[64,512]{1,0:T(8,128)(2,1)} copy(bf16[64,512]{1,0:T(8,128)(2,1)} %get-tuple-element.4) | data formatting | bytes 131072
  112.3 2.3 %copy.9 = bf16[512,1024]{1,0:T(8,128)(2,1)} copy(bf16[512,1024]{1,0:T(8,128)(2,1)} %get-tuple-element.5) | data formatting | bytes 2097152

commit v3 on v2

--- a/solution.py
+++ b/solution.py
@@ -45,10 +45,10 @@
 
 
 def kernel(
-    x_ref, code_ref, cons_ref, out_ref,
+    x_ref, window_ref, label_ref, edge_ref, cons_ref, out_ref,
     unit, send, own, sib, ret, acc, msend, mplane, mz, mz_sib, ztab,
-    edge_send, edge_own, edge_sib, ecode_send, ecode_own, ecode_sib, num, num_sib, cnt, cnt_sib, dens, lab_col,
-    line_a, line_b, row_ssem, row_sem, ret_ssem, ret_sem, mp_ssem, mp_sem, mz_ssem, mz_sem,
+    edge_send, edge_in, ecode_send, ecode_in, num, num_sib, dens, lab_col, picks,
+    plane_sem, row_ssem, row_sem, ret_ssem, ret_sem, mp_ssem, mp_sem, mz_ssem, mz_sem,
     pair_ssem, pair_sem, edge_ssem, edge_sem, zt_ssem, zt_sem, zp_ssem, zp_sem,
 ):
     me = lax.axis_index("mass")
@@ -71,12 +71,12 @@
     barrier = pltpu.get_barrier_semaphore()
     for k in range(1, 8):
         signal(barrier, chip(0, k, 0), rep)
-    for k in range(1, 4):
-        signal(barrier, chip(k, 0, 0), rep)
-        signal(barrier, chip(0, 0, k), rep)
+    for p in range(1, 16):
+        signal(barrier, chip(p // 4, 0, p % 4), rep)
     signal(barrier, me, other)
-
-    code_row = code_ref[...]
+    signal(barrier, (me + 1) % n, other)
+
+    code_row = window_ref[...] * 8192 + label_ref[...] * 128 + edge_ref[...] + 1
     diag = iota((rows, rows), 0) == iota((rows, rows), 1)
     code_col = jnp.sum(jnp.where(diag, code_row.astype(F32), 0.0), axis=1, keepdims=True).astype(jnp.int32)
 
@@ -100,16 +100,8 @@
     slot_row = (plane_row * 8 + order_row) * SLOTS + rank_row
     slot_col = (order_col * 16 + plane_col) * SLOTS + rank_col
 
-    pl.semaphore_wait(barrier, 14)
-    for k in range(1, 4):
-        signal(line_a, chip(0, 0, k), rep)
-
     wide = x_ref[...].astype(F32)
     unit[...] = (wide * lax.rsqrt(jnp.mean(wide * wide, axis=1, keepdims=True) + 1e-6)).astype(BF16)
-
-    pl.semaphore_wait(line_a, 3)
-    for k in range(1, 4):
-        signal(line_b, chip(k, 0, 0), rep)
 
     lane = iota((rows, 128), 1) - ((w_col >> 2) & 7) * 16
     code2 = jnp.where(lane == rank_col, l_col + 1, 0) + jnp.where(lane == rank_col + SLOTS, e_col, 0)
@@ -121,7 +113,9 @@
         send[pl.ds(32 * c, 32)] = mm(pick, unit[...]).reshape(32, SLOTS, 1024).astype(BF16)
 
     pack(0)
-    pl.semaphore_wait(line_b, 3)
+    pl.semaphore_wait(barrier, 24)
+    for p in range(1, 16):
+        signal(plane_sem, chip(p // 4, 0, p % 4), rep)
 
     def plane_copy(p, sign):
         return remote(msend.at[p], mplane.at[p], mp_ssem, mp_sem, chip(sign * (p // 4), 0, sign * (p % 4)), rep)
@@ -131,27 +125,39 @@
     for p in range(1, 16):
         plane_copy(p, 1).start()
 
+    def send_block(p, j, group):
+        d = p * 8 + j
+        remote(send.at[d], own.at[d], row_ssem, row_sem.at[group], chip(p // 4, depth_of(j), p % 4), rep).start()
+
+    @pl.loop(1, 8)
+    def _(j):
+        send_block(0, j, 0)
+
+    for c in range(1, 4):
+        pack(c)
+    for g, (begin, count) in enumerate(GROUPS):
+        @pl.loop(max(1, begin // 8), (begin + count) // 8)
+        def _(p):
+            send_block(p, 0, g)
+
+    pl.semaphore_wait(plane_sem, 15)
+
     def send_rows(group):
         begin, count = GROUPS[group]
-
-        @pl.loop(max(1, begin), begin + count)
-        def _(d):
-            p = d // 8
-            m = chip(p // 4, depth_of(d % 8), p % 4)
-            remote(send.at[d], own.at[d], row_ssem, row_sem.at[group], m, rep).start()
+        first = max(1, begin // 8)
+
+        @pl.loop(0, 7 * ((begin + count) // 8 - first))
+        def _(i):
+            send_block(first + i // 7, 1 + i % 7, group)
 
     send_rows(0)
-    for c in range(1, 4):
-        pack(c)
-    send_rows(1)
 
     pltpu.make_async_copy(msend, mplane, mp_sem).wait()
     mz[0] = mplane[...].reshape(16, 128).astype(BF16)
     for j in range(1, 8):
         remote(mz.at[0], mz.at[j], mz_ssem.at[j], mz_sem.at[j], chip(0, ZO[j], 0), rep).start()
+    send_rows(1)
     send_rows(2)
-    send_rows(3)
-    send_rows(4)
 
     def pair(src, dst, k):
         return remote(src, dst, pair_ssem.at[k], pair_sem.at[k], me, other)
@@ -179,11 +185,27 @@
     ecode = jnp.sum(jnp.where(iota((n, n), 1) == z * 16 + SLOTS, blocks, 0.0), axis=1, keepdims=True)
     ecode_send[...] = jnp.broadcast_to(ecode, (n, 128)).astype(BF16)
     below = (me + n - 1) % n
-    edge_code_copy = remote(ecode_send, ecode_own, edge_ssem.at[5], edge_sem.at[5], below, rep)
-    edge_code_copy.start()
+    edge_codes = [
+        remote(ecode_send, ecode_in.at[k], edge_ssem.at[k, 5], edge_sem.at[k, 5], below, r)
+        for k, r in enumerate((rep, other))
+    ]
+    for copy in edge_codes:
+        copy.start()
     pair_meta.wait()
     _, _, row_sib = label_forms(mz_sib[...].reshape(n, 128))
     dens[...] = jnp.zeros((n * SLOTS, 1), F32)
+    cluster = iota((CLUSTERS, n * SLOTS), 0) + 1
+    member = onehot(cluster == row_own.astype(jnp.int32))
+    also = onehot(cluster == row_sib.astype(jnp.int32))
+    count_all = jnp.sum(member.astype(F32) + also.astype(F32), axis=1, keepdims=True)
+
+    plane_i = iota((16 * SLOTS, 128), 0)
+    plane_c = iota((16 * SLOTS, 128), 1)
+    codes = mm(onehot(iota((16 * SLOTS, 16), 1) == iota((16 * SLOTS, 16), 0) >> 3), mz[0])
+    for j in range(8):
+        at = ((z + ZO[j]) % 8) * 16
+        labels = jnp.sum(jnp.where(plane_c == (plane_i & 7) + at, codes, 0.0), axis=1, keepdims=True)
+        picks[j] = onehot(iota((16 * SLOTS, CLUSTERS), 1) + 1 == labels.astype(jnp.int32))
 
     def flat(ref, begin, end):
         return ref[pl.ds(begin, end - begin)].reshape((end - begin) * SLOTS, 1024)
@@ -204,7 +226,12 @@
     def group_edge(g):
         begin, count = GROUPS[g]
         part = pl.ds(begin, count)
-        return remote(edge_send.at[part], edge_own.at[part], edge_ssem.at[g], edge_sem.at[g], below, rep)
+        return remote(edge_send.at[part], edge_in.at[0, part], edge_ssem.at[0, g], edge_sem.at[0, g], below, rep)
+
+    def pass_edge(g):
+        begin, count = GROUPS[g]
+        part = pl.ds(begin, count)
+        return remote(edge_in.at[0, part], edge_in.at[1, part], edge_ssem.at[1, g], edge_sem.at[1, g], me, other)
 
     def arrive(g):
         begin, count = GROUPS[g]
@@ -223,6 +250,8 @@
         add_density(begin, end, flat(own, 0, end), row_own[:, seen])
         if begin:
             add_density(0, begin, flat(own, begin, end), row_own[:, new])
+        group_edge(g).wait()
+        pass_edge(g).start()
         group_pair(g).wait()
         add_density(begin, end, flat(sib, 0, end), row_sib[:, seen])
         if begin:
@@ -230,42 +259,34 @@
 
     for g in range(len(GROUPS)):
         arrive(g)
+        if g + 3 < len(GROUPS):
+            send_rows(g + 3)
         if g:
             process(g - 1)
+    process(len(GROUPS) - 1)
+    for copy in edge_codes:
+        copy.wait()
+    edge_row = jnp.where(
+        me < n - 1,
+        mm_nt(onehot(iota((8, 128), 1) == 0), ecode_in[...].reshape(2 * n, 128))[0:1], 0.0)
     for g in range(len(GROUPS)):
-        group_edge(g).wait()
-    edge_code_copy.wait()
-    relay = [pair(edge_own, edge_sib, 6), pair(ecode_own, ecode_sib, 7)]
-    for copy in relay:
-        copy.start()
-    process(len(GROUPS) - 1)
-    for copy in relay:
-        copy.wait()
-    live = me < n - 1
-
-    def edge_labels(ref):
-        return jnp.where(live, mm_nt(onehot(iota((8, 128), 1) == 0), ref[...])[0:1], 0.0)
-
-    add_density(0, n, edge_own[...], edge_labels(ecode_own))
-    add_density(0, n, edge_sib[...], edge_labels(ecode_sib))
+        pass_edge(g).wait()
+    add_density(0, n, edge_in[...].reshape(2 * n, 1024), edge_row)
 
     weighted = (dens[...] * flat(own, 0, n).astype(F32)).astype(BF16)
-    member = onehot(iota((CLUSTERS, n * SLOTS), 0) + 1 == row_own.astype(jnp.int32))
     num[...] = mm(member, weighted)
-    cnt[...] = jnp.broadcast_to(jnp.sum(member.astype(F32), axis=1, keepdims=True), (CLUSTERS, 128))
-    pair_num = [pair(num, num_sib, 8), pair(cnt, cnt_sib, 9)]
-    for copy in pair_num:
-        copy.start()
+    pair_num = pair(num, num_sib, 6)
+    pair_num.start()
     remote(send.at[pl.ds(0, n - 1)], own.at[pl.ds(0, n - 1)], row_ssem, row_sem.at[0], me, other).wait_send()
     remote(msend.at[pl.ds(0, 15)], mplane.at[pl.ds(0, 15)], mp_ssem, mp_sem, me, other).wait_send()
-    for copy in pair_num:
-        copy.wait()
-    ztab[0] = ((num[...] + num_sib[...]) / (cnt[:, 0:1] + cnt_sib[:, 0:1] + 1.0)).astype(BF16)
+    pair_num.wait()
+    ztab[0] = ((num[...] + num_sib[...]) / (count_all + 1.0)).astype(BF16)
 
     half = pl.ds(pl.multiple_of(rep * 32, 32), 32)
 
     def table_copy(j):
-        return remote(ztab.at[0, half], ztab.at[j, half], zt_ssem.at[j], zt_sem.at[j], chip(0, -ZO[j], 0), rep)
+        src, dst = (ztab.at[0], ztab.at[j]) if j < 3 else (ztab.at[0, half], ztab.at[j, half])
+        return remote(src, dst, zt_ssem.at[j], zt_sem.at[j], chip(0, -ZO[j], 0), rep)
 
     def table_pair(j):
         return remote(ztab.at[j, half], ztab.at[j, half], zp_ssem.at[j], zp_sem.at[j], me, other)
@@ -274,15 +295,8 @@
         table_copy(j).start()
     cons_ref[...] = ztab[0, :, pl.ds(pl.multiple_of(rep * 512, 512), 512)]
 
-    plane_i = iota((16 * SLOTS, 128), 0)
-    plane_c = iota((16 * SLOTS, 128), 1)
-    codes = mm(onehot(iota((16 * SLOTS, 16), 1) == plane_i[:, 0:16] >> 3), mz[0])
-
     def answer(j):
-        at = ((z + ZO[j]) % 8) * 16
-        labels = jnp.sum(jnp.where(plane_c == (plane_i & 7) + at, codes, 0.0), axis=1, keepdims=True)
-        pick = onehot(iota((16 * SLOTS, CLUSTERS), 1) + 1 == labels.astype(jnp.int32))
-        send[pl.ds(16 * j, 16)] = mm(pick, ztab[j]).reshape(16, SLOTS, 1024).astype(BF16)
+        send[pl.ds(16 * j, 16)] = mm(picks[j], ztab[j]).reshape(16, SLOTS, 1024).astype(BF16)
         pltpu.make_async_copy(send.at[16 * j], ret.at[16 * j], ret_sem.at[j // 2]).start()
 
         @pl.loop(1, 16)
@@ -291,17 +305,20 @@
                    chip(-(p // 4), 0, -(p % 4)), rep).start()
 
     for j in range(8):
-        if j < 7:
-            table_copy(j + 1).wait_recv()
-            table_pair(j + 1).start()
-        if j:
+        if j in (1, 2):
+            table_copy(j).wait_recv()
+        elif j:
             table_pair(j).wait_recv()
         answer(j)
+        k = j + 2
+        if 3 <= k < 8:
+            table_copy(k).wait_recv()
+            table_pair(k).start()
 
     for q in range(4):
         part = pl.ds(32 * q, 32)
+        pick = onehot(iota((rows, 256), 1) + 256 * q == slot_col)
         pltpu.make_async_copy(send.at[part], ret.at[part], ret_sem.at[q]).wait()
-        pick = onehot(iota((rows, 256), 1) + 256 * q == slot_col)
         got = mm(pick, ret[part].reshape(256, 1024))
         if q == 0:
             acc[...] = got
@@ -311,40 +328,52 @@
             out_ref[...] = (acc[...] + got).astype(BF16)
     for j in range(1, 8):
         table_copy(j).wait_send()
-        table_pair(j).wait_send()
+        if j >= 3:
+            table_pair(j).wait_send()
     remote(send.at[pl.ds(0, 120)], ret.at[pl.ds(0, 120)], ret_ssem, ret_sem.at[0], me, other).wait_send()
 
 
 def body(spectra, window, labels, edge_labels):
     rows, dim = spectra.shape
     n = lax.axis_size("mass")
-    code = (window * 8192 + labels * 128 + edge_labels + 1).reshape(1, rows)
     vm = lambda shape, t=BF16: pltpu.VMEM(shape, t)
     block = (n, SLOTS, dim)
     dma = pltpu.SemaphoreType.DMA
     regular = pltpu.SemaphoreType.REGULAR
-    return pl.pallas_call(
+    cons, assigned = pl.pallas_call(
         kernel,
         out_shape=(
             jax.ShapeDtypeStruct((CLUSTERS, dim // 2), BF16),
             jax.ShapeDtypeStruct((rows, dim), BF16),
         ),
-        in_specs=[pl.BlockSpec(memory_space=pltpu.VMEM)] * 2,
+        in_specs=[pl.BlockSpec(memory_space=pltpu.VMEM)] * 4,
         out_specs=(pl.BlockSpec(memory_space=pltpu.VMEM), pl.BlockSpec(memory_space=pltpu.VMEM)),
         scratch_shapes=[
             vm((rows, dim)), vm(block), vm(block), vm(block), vm(block), vm((rows, dim), F32),
             vm((16, 1, 128), F32), vm((16, 1, 128), F32), vm((8, 16, 128)), vm((8, 16, 128)), vm((8, CLUSTERS, dim)),
-            vm((n, dim)), vm((n, dim)), vm((n, dim)), vm((n, 128)), vm((n, 128)), vm((n, 128)),
-            vm((CLUSTERS, dim), F32), vm((CLUSTERS, dim), F32), vm((CLUSTERS, 128), F32), vm((CLUSTERS, 128), F32),
-            vm((n * SLOTS, 1), F32), vm((n * SLOTS, 1), F32),
-            regular, regular, dma, dma((5,)), dma, dma((4,)), dma, dma, dma((8,)), dma((8,)),
-            dma((10,)), dma((10,)), dma((6,)), dma((6,)), dma((8,)), dma((8,)), dma((8,)), dma((8,)),
+            vm((n, dim)), vm((2, n, dim)), vm((n, 128)), vm((2, n, 128)),
+            vm((CLUSTERS, dim), F32), vm((CLUSTERS, dim), F32), vm((n * SLOTS, 1), F32), vm((n * SLOTS, 1), F32),
+            vm((8, 16 * SLOTS, CLUSTERS)),
+            regular, dma, dma((5,)), dma, dma((4,)), dma, dma, dma((8,)), dma((8,)),
+            dma((7,)), dma((7,)), dma((2, 6)), dma((2, 6)), dma((8,)), dma((8,)), dma((8,)), dma((8,)),
         ],
         compiler_params=pltpu.CompilerParams(
             collective_id=0, has_side_effects=True, vmem_limit_bytes=56 * 1024 * 1024),
         cost_estimate=pl.CostEstimate(flops=8 * 10**9, bytes_accessed=4 * 10**6, transcendentals=2 * 10**6),
         name="consensus",
-    )(spectra, code)
+    )(spectra, window.reshape(1, rows), labels.reshape(1, rows), edge_labels.reshape(1, rows))
+    return pl.pallas_call(
+        place,
+        out_shape=(jax.ShapeDtypeStruct(cons.shape, BF16), jax.ShapeDtypeStruct(assigned.shape, BF16)),
+        in_specs=[pl.BlockSpec(memory_space=pltpu.VMEM)] * 2,
+        out_specs=(pl.BlockSpec(memory_space=pltpu.VMEM), pl.BlockSpec(memory_space=pltpu.VMEM)),
+        name="place",
+    )(cons, assigned)
+
+
+def place(a_ref, b_ref, c_ref, d_ref):
+    c_ref[...] = a_ref[...]
+    d_ref[...] = b_ref[...]
 
 
 def solution(mesh):

time: 115 us -> 110 us (0.957)
  local copies, waits for them, and re-layouts: 3.74 us -> 0 us
  other arithmetic: 1.3 us -> 0 us
    unnamed x2 -> x0, local copies, waits for them, and re-layouts: 3.74 us -> none
    pallas_call x1, Pallas kernels: 109 us -> 106 us  [body(): pl.pallas_call(kernel, out_shape=(jax.ShapeDtypeStruct((CLUSTERS, dim //...]
    pallas_call x0 -> x1, Pallas kernels: none -> 2.31 us  [body(): pl.pallas_call(place, out_shape=(jax.ShapeDtypeStruct(cons.shape, BF16),...]
    add x1 -> x0, other arithmetic: 1.3 us -> none  [body(): code = (window * 8192 + labels * 128 + edge_labels + 1).reshape(1, rows)]
where the time goes in v3:
time: 110 us; the launch traced here: 109 us
  Pallas kernels  109 us (99%)
    pallas_call x1, Pallas kernels, body(): pl.pallas_call(kernel, out_shape=(jax.ShapeDtypeStruct((CLUSTERS, dim //...  106 us
    pallas_call x1, Pallas kernels, body(): pl.pallas_call(place, out_shape=(jax.ShapeDtypeStruct(cons.shape, BF16),...  2.31 us

profile of v3, /device:TPU:1, one launch (start us, length us, event | category | flops | bytes accessed | tf_op | source)
XLA Modules:
  0.0 109.4 jit_solution(12918539274422264653)
XLA Ops:
  0.6 106.5 %consensus.1 = (bf16[64,512]{1,0:T(8,128)(2,1)}, bf16[512,1024]{1,0:T(8,128)(2,1)}) custom-call(bf16[512,1024]{1,0:T(8,128)(2,1)} %x_ref.1, s32[1,512]{1,0:T(1,128)} %bitcast.3, s32[1,512]{1,0:T(1,128)} %bitcast.4, s32[1,512]{1,0:T(1,128)} %bitcast.5), custom_call_target="tpu_custom_call" | custom-call | flops 8000000000 | bytes 4000000 | tf_op jit(solution)/shard_map/consensus/pallas_call | solution.py:343
  107.1 2.3 %place.1 = (bf16[64,512]{1,0:T(8,128)(2,1)}, bf16[512,1024]{1,0:T(8,128)(2,1)}) custom-call(bf16[64,512]{1,0:T(8,128)(2,1)} %get-tuple-element.4.a_ref, bf16[512,1024]{1,0:T(8,128)(2,1)} %get-tuple-element.5.b_ref), custom_call_target="tpu_custom_call" | custom-call | tf_op jit(solution)/shard_map/place/pallas_call | solution.py:365

commit v4 on v3

--- a/solution.py
+++ b/solution.py
@@ -273,14 +273,20 @@
         pass_edge(g).wait()
     add_density(0, n, edge_in[...].reshape(2 * n, 1024), edge_row)
 
-    weighted = (dens[...] * flat(own, 0, n).astype(F32)).astype(BF16)
-    num[...] = mm(member, weighted)
-    pair_num = pair(num, num_sib, 6)
-    pair_num.start()
+    sums = []
+    for h in range(2):
+        lanes = pl.ds(512 * h, 512)
+        weighted = (dens[...] * own[:, :, lanes].reshape(n * SLOTS, 512).astype(F32)).astype(BF16)
+        num[:, lanes] = mm(member, weighted)
+        copy = pair(num.at[:, lanes], num_sib.at[:, lanes], 6 + h)
+        copy.start()
+        sums.append(copy)
     remote(send.at[pl.ds(0, n - 1)], own.at[pl.ds(0, n - 1)], row_ssem, row_sem.at[0], me, other).wait_send()
     remote(msend.at[pl.ds(0, 15)], mplane.at[pl.ds(0, 15)], mp_ssem, mp_sem, me, other).wait_send()
-    pair_num.wait()
-    ztab[0] = ((num[...] + num_sib[...]) / (count_all + 1.0)).astype(BF16)
+    for h, copy in enumerate(sums):
+        lanes = pl.ds(512 * h, 512)
+        copy.wait()
+        ztab[0, :, lanes] = ((num[:, lanes] + num_sib[:, lanes]) / (count_all + 1.0)).astype(BF16)
 
     half = pl.ds(pl.multiple_of(rep * 32, 32), 32)
 
@@ -355,7 +361,7 @@
             vm((CLUSTERS, dim), F32), vm((CLUSTERS, dim), F32), vm((n * SLOTS, 1), F32), vm((n * SLOTS, 1), F32),
             vm((8, 16 * SLOTS, CLUSTERS)),
             regular, dma, dma((5,)), dma, dma((4,)), dma, dma, dma((8,)), dma((8,)),
-            dma((7,)), dma((7,)), dma((2, 6)), dma((2, 6)), dma((8,)), dma((8,)), dma((8,)), dma((8,)),
+            dma((8,)), dma((8,)), dma((2, 6)), dma((2, 6)), dma((8,)), dma((8,)), dma((8,)), dma((8,)),
         ],
         compiler_params=pltpu.CompilerParams(
             collective_id=0, has_side_effects=True, vmem_limit_bytes=56 * 1024 * 1024),

time: 110 us -> 110 us (level)
  no operation moved by 1% of the time
where the time goes in v4:
time: 110 us; the launch traced here: 109 us
  Pallas kernels  109 us (99%)
    pallas_call x1, Pallas kernels, body(): pl.pallas_call(kernel, out_shape=(jax.ShapeDtypeStruct((CLUSTERS, dim //...  106 us
    pallas_call x1, Pallas kernels, body(): pl.pallas_call(place, out_shape=(jax.ShapeDtypeStruct(cons.shape, BF16),...  2.31 us

profile of v4, /device:TPU:1, one launch (start us, length us, event | category | flops | bytes accessed | tf_op | source)
XLA Modules:
  0.0 109.4 jit_solution(822532364768031679)
XLA Ops:
  0.6 106.5 %consensus.1 = (bf16[64,512]{1,0:T(8,128)(2,1)}, bf16[512,1024]{1,0:T(8,128)(2,1)}) custom-call(bf16[512,1024]{1,0:T(8,128)(2,1)} %x_ref.1, s32[1,512]{1,0:T(1,128)} %bitcast.3, s32[1,512]{1,0:T(1,128)} %bitcast.4, s32[1,512]{1,0:T(1,128)} %bitcast.5), custom_call_target="tpu_custom_call" | custom-call | flops 8000000000 | bytes 4000000 | tf_op jit(solution)/shard_map/consensus/pallas_call | solution.py:349
  107.1 2.3 %place.1 = (bf16[64,512]{1,0:T(8,128)(2,1)}, bf16[512,1024]{1,0:T(8,128)(2,1)}) custom-call(bf16[64,512]{1,0:T(8,128)(2,1)} %get-tuple-element.4.a_ref, bf16[512,1024]{1,0:T(8,128)(2,1)} %get-tuple-element.5.b_ref), custom_call_target="tpu_custom_call" | custom-call | tf_op jit(solution)/shard_map/place/pallas_call | solution.py:371
